TPU v7x, 512 devices: a whole 4x8x8 slice. The times are simulated.
512 devices in a mesh: ra: 128 (over z_hi, x, y), slab: 4 (over z_lo, core).
Axes of the slice: x: 4, y: 8, z: 8 (z_hi: 4, z_lo: 2; z = z_hi * 2 + z_lo), core: 2. Of those that a mesh axis runs over, the one named last changes fastest.
Arguments:
- images: bfloat16 [512, 256, 1024], P('ra', 'slab'), may hold values from -6 to 6
- row_taps: bfloat16 [20, 41], replicated, may hold values from -1 to 1
- col_taps: bfloat16 [20, 41], replicated, may hold values from -1 to 1
- coef: float32 [512, 4, 20], replicated, may hold values from -1.25 to 1.25
- blocks: int32 [512, 8], replicated, may hold values from 0 to 3
- boxes: int32 [512, 2], replicated, may hold values from 0 to 8, as said below
- ivar: float32 [512], replicated, may hold values from 0.25 to 4
- counts: int32 [128], replicated, may hold values from 1 to 4, as said below
Outputs:
- coadd: float32 [256, 65536], P('slab', 'ra')
Inputs may be any that keep to these rules, and one draw needn't show every extreme that they name: boxes[v, 0] lies below 4 and boxes[v, 1] above it, so every piece crosses from its home patch into the next; both ends are reached. Slots 0 to counts[p] - 1 of home patch p are live; some patch holds 4.
All inputs are finite; a program needn't handle non-finite values.
Results may differ from a plain program's by a relative error of at most 0.0029.
Values may be sent and summed in bfloat16 or wider, within the bound.
A program may use at most 64 MiB of HBM per device.

v0:
```python
import functools

import jax
import jax.numpy as jnp
from jax import lax
from jax.experimental import pallas as pl
from jax.experimental.pallas import tpu as pltpu
from jax.sharding import PartitionSpec as P

MESH = pl.DeviceIdType.MESH
NB = 20
TAPS = 41
SETS = 4
REACH = 20
SLOTS = 4
ROWS = 64
EDGE = 32
NEAR = 24
WHOLE = 16
REST = REACH - WHOLE
TILE = 128
TILES = 8
HALF = 4
WIDE = HALF * TILE
F32 = jnp.float32
BF16 = jnp.bfloat16


def kernel(npatch, nslab, images, row_taps_in, col_taps_in, coef, blocks, boxes_in, ivar_in, counts_in,
           out, row_taps, col_taps, boxes, ivar, counts, window, coef_v, block_v, row_mat, col_mat, factor, mixed, far_out, far_in, edge_out, edge_in, near_out, near_in,
           tile_sem, local_sem, far_send, far_recv, near_send, near_recv):
    patch = lax.axis_index("ra")
    slab = lax.axis_index("slab")
    after = lax.rem(patch + 1, npatch)
    before = lax.rem(patch + npatch - 1, npatch)
    has_up = slab > 0
    has_down = slab < nslab - 1

    barrier = pltpu.get_barrier_semaphore()

    def greet(p, s):
        pl.semaphore_signal(barrier, inc=1, device_id=(p, s), device_id_type=MESH)

    tiles = [pltpu.make_async_copy(images.at[:, :, pl.ds(t * TILE, TILE)], window.at[t, :, :, pl.ds(0, TILE)],
                                   tile_sem.at[t]) for t in range(TILES)]
    lane_block = pl.ds(pl.multiple_of((patch * SLOTS // TILE) * TILE, TILE), TILE)
    small = [(col_taps_in, col_taps), (row_taps_in, row_taps), (boxes_in, boxes), (ivar_in, ivar), (counts_in, counts),
             (coef.at[:, :, lane_block], coef_v), (blocks.at[:, lane_block], block_v)]
    tables = [pltpu.make_async_copy(src, dst, local_sem.at[i]) for i, (src, dst) in enumerate(small)]
    for copy in tables[:2] + tiles[:HALF - 2:-1] + tables[2:] + tiles[HALF - 2::-1]:
        copy.start()

    greet(before, slab)

    @pl.when(has_up)
    def _():
        greet(before, slab - 1)
        greet(patch, slab - 1)

    @pl.when(has_down)
    def _():
        greet(before, slab + 1)
        greet(patch, slab + 1)

    tap = lax.broadcasted_iota(jnp.int32, (TAPS, TILE), 0)
    lane = lax.broadcasted_iota(jnp.int32, (TAPS, TILE), 1)

    def laid(taps, at):
        return jnp.dot(taps[...], (lane == at).astype(F32).astype(BF16), preferred_element_type=F32)

    def rolled(base, b):
        band = jnp.broadcast_to(base[b:b + 1, :], (TILE, TILE))
        return pltpu.roll(band, 0, 1, stride=1, stride_axis=0)

    row_at = lax.broadcasted_iota(jnp.int32, (TILE, TILE), 0)
    col_at = lax.broadcasted_iota(jnp.int32, (TILE, TILE), 1)
    close = jnp.abs(row_at - col_at) <= REACH
    low_half = col_at < ROWS
    for copy in tables + tiles[HALF - 1:]:
        copy.wait()
    col_base = laid(col_taps, lax.rem(REACH - tap + TILE, TILE))
    even_base = laid(row_taps, tap + (TILE - EDGE - REACH))
    odd_base = laid(row_taps, tap + (ROWS - EDGE - REACH))

    def build(pair):
        for b in (2 * pair, 2 * pair + 1):
            band = rolled(col_base, b)
            col_mat[0:TILE, b * TILE:(b + 1) * TILE] = jnp.where(close, band, 0.0).astype(BF16)
            col_mat[TILE:, b * TILE:(b + 1) * TILE] = jnp.where(close, 0.0, band).astype(BF16)
        both = jnp.where(low_half, rolled(even_base, 2 * pair), rolled(odd_base, 2 * pair + 1))
        row_mat[:, pair * TILE:(pair + 1) * TILE] = both.astype(BF16)

    def visit_scalars(home, v):
        visit = home * SLOTS + v
        scale = jnp.where(v < counts[home], ivar[visit], 0.0)
        inside = [jnp.where((t >= boxes[0, visit]) & (t < boxes[1, visit]), 1.0, 0.0) for t in range(TILES)]
        return scale, inside

    own = [visit_scalars(patch, v) for v in range(SLOTS)]
    turn = lax.rem(TILE - lax.rem(patch * SLOTS, TILE), TILE)
    sets = [pltpu.roll(coef_v[:, s, :], turn, 1) for s in range(SETS)]
    block = pltpu.roll(block_v[...], turn, 1)

    def factors(first):
        for t in range(first, first + HALF):
            pick = block[t:t + 1, :]
            chosen = jnp.zeros((NB, TILE), F32)
            for s in range(SETS):
                chosen = chosen + jnp.where(pick == s, sets[s], 0.0)
            for v in range(SLOTS):
                scale, inside = own[v]
                factor[t, v, 0:NB, :] = jnp.broadcast_to(chosen[:, v:v + 1], (NB, TILE)) * (scale * inside[t])

    factors(HALF)

    @pl.when(jnp.logical_not(has_up))
    def _():
        edge_in[0] = jnp.zeros((WHOLE, WIDE + TILE), BF16)
        near_in[0:NEAR, :] = jnp.zeros((NEAR, WIDE), F32)

    @pl.when(jnp.logical_not(has_down))
    def _():
        edge_in[1] = jnp.zeros((WHOLE, WIDE + TILE), BF16)
        near_in[NEAR:, :] = jnp.zeros((NEAR, WIDE), F32)

    low = lax.broadcasted_iota(jnp.int32, (ROWS, TILE), 1) < TILE // 2

    def beside(t):
        for v in range(SLOTS):
            right = window[t + 1, v, :, 0:TILE] if t + 1 < TILES else jnp.zeros((ROWS, TILE), BF16)
            left = window[t - 1, v, :, 0:TILE] if t > 0 else jnp.zeros((ROWS, TILE), BF16)
            inside = own[v][1]
            keep = jnp.where(low, inside[t + 1] if t + 1 < TILES else 0.0, inside[t - 1] if t > 0 else 0.0)
            window[t, v, :, TILE:] = jnp.where(low, right, left) * keep.astype(BF16)

    def spread(first):
        for t in range(first, first + HALF):
            beside(t)

    def filtered(first, pairs, fresh):
        block_rows = window[first:first + HALF].reshape(HALF * SLOTS * ROWS, 2 * TILE)
        for pair in pairs:
            if fresh:
                build(pair)
            part = jnp.dot(block_rows, col_mat[:, pair * 2 * TILE:(pair + 1) * 2 * TILE], preferred_element_type=F32)
            for t in range(HALF):
                for w in range(2):
                    b = 2 * pair + w
                    total = None
                    for v in range(SLOTS):
                        at = (t * SLOTS + v) * ROWS
                        term = part[at:at + ROWS, w * TILE:(w + 1) * TILE] * factor[first + t, v, b:b + 1, :]
                        total = term if total is None else total + term
                    mixed[b * ROWS:(b + 1) * ROWS, t * TILE:(t + 1) * TILE] = total.astype(BF16)

    def row_product():
        return jnp.dot(row_mat[...], mixed[...], preferred_element_type=F32)

    def far_copy(i, p, s, src, dst):
        return pltpu.make_async_remote_copy(
            src_ref=src, dst_ref=dst, send_sem=far_send.at[i], recv_sem=far_recv.at[i],
            device_id=(p, s), device_id_type=MESH)

    far_same = far_copy(0, after, slab, far_out, far_in)
    far_up = far_copy(1, after, slab - 1, edge_out.at[0], edge_in.at[1])
    far_down = far_copy(2, after, slab + 1, edge_out.at[1], edge_in.at[0])

    def near_copy(i, s, src, dst):
        return pltpu.make_async_remote_copy(
            src_ref=near_out.at[pl.ds(src, NEAR), :], dst_ref=near_in.at[pl.ds(dst, NEAR), :],
            send_sem=near_send.at[i], recv_sem=near_recv.at[i], device_id=(patch, s), device_id_type=MESH)

    near_up = near_copy(0, slab - 1, 0, NEAR)
    near_down = near_copy(1, slab + 1, NEAR, 0)

    def send_to(target):
        if target != 1:
            @pl.when(slab == target)
            def _():
                far_same.start()

        @pl.when(slab == target + 1)
        def _():
            far_up.start()

        @pl.when(slab == target - 1)
        def _():
            far_down.start()

    spread(HALF)
    filtered(HALF, range(NB // 2), True)
    far = row_product()
    far_out[...] = far[EDGE:EDGE + ROWS].astype(BF16)

    links = has_up.astype(jnp.int32) + has_down.astype(jnp.int32)
    pl.semaphore_wait(barrier, 1 + 2 * links)

    @pl.when(slab == 1)
    def _():
        far_same.start()

    def edge(at, rest):
        last = [far[rest:rest + REST, t * TILE:(t + 1) * TILE] for t in range(HALF)]
        return jnp.concatenate([far[at:at + WHOLE], jnp.concatenate(last, axis=0)], axis=1).astype(BF16)

    edge_out[0] = edge(EDGE - WHOLE, EDGE - REACH)
    edge_out[1] = edge(EDGE + ROWS, EDGE + ROWS + WHOLE)
    send_to(1)
    for t in range(HALF - 1):
        tiles[t].wait()
    factors(0)
    spread(0)
    filtered(0, range(0, 3), False)
    send_to(2)
    send_to(3)
    filtered(0, range(3, 10), False)
    send_to(0)
    home = row_product()
    near_out[0:NEAR, :] = home[EDGE - NEAR:EDGE]
    near_out[NEAR:, :] = home[EDGE + ROWS:EDGE + ROWS + NEAR]

    @pl.when(has_up)
    def _():
        near_up.start()

    @pl.when(has_down)
    def _():
        near_down.start()

    other = [visit_scalars(before, v) for v in range(SLOTS)]
    shares = []
    for t in range(HALF):
        weight = jnp.float32(0.0)
        for v in range(SLOTS):
            weight = weight + own[v][0] * own[v][1][t] + other[v][0] * other[v][1][t + HALF]
        shares.append(1.0 / jnp.full((ROWS, TILE), jnp.maximum(weight, 1.0), F32))

    @pl.when(has_up)
    def _():
        near_down.wait_recv()

    @pl.when(has_down)
    def _():
        near_up.wait_recv()

    out[0:NEAR, :] = home[EDGE:EDGE + NEAR] + near_in[0:NEAR, :]
    out[NEAR:ROWS - NEAR, :] = home[EDGE + NEAR:EDGE + ROWS - NEAR]
    out[ROWS - NEAR:, :] = home[EDGE + ROWS - NEAR:EDGE + ROWS] + near_in[NEAR:, :]

    @pl.when(has_up)
    def _():
        far_down.wait_recv()

    @pl.when(has_down)
    def _():
        far_up.wait_recv()

    far_same.wait_recv()
    for t in range(HALF):
        span = slice(t * TILE, (t + 1) * TILE)
        rest = slice(t * REST, (t + 1) * REST)
        ends = edge_in[:, :, span].astype(F32)
        last = edge_in[:, :, WIDE:].astype(F32)
        gap = jnp.zeros((ROWS - 2 * REACH, TILE), F32)
        edges = jnp.concatenate([ends[0], last[0, rest], gap, last[1, rest], ends[1]], axis=0)
        out[:, span] = (out[:, span] + (far_in[:, span].astype(F32) + edges)) * shares[t]

    far_same.wait_send()

    @pl.when(has_up)
    def _():
        far_up.wait_send()
        near_up.wait_send()

    @pl.when(has_down)
    def _():
        far_down.wait_send()
        near_down.wait_send()


def local_part(npatch, nslab, images, row_taps, col_taps, coef, blocks, boxes, ivar, counts):
    vmem = pl.BlockSpec(memory_space=pltpu.VMEM)
    anyplace = pl.BlockSpec(memory_space=pl.ANY)
    dma = pltpu.SemaphoreType.DMA
    return pl.pallas_call(
        functools.partial(kernel, npatch, nslab),
        out_shape=pltpu.VMEM((ROWS, WIDE), F32),
        in_specs=[anyplace] * 8,
        out_specs=vmem,
        scratch_shapes=[
            pltpu.VMEM(row_taps.shape, BF16),
            pltpu.VMEM(col_taps.shape, BF16),
            pltpu.SMEM(boxes.shape[::-1], jnp.int32),
            pltpu.SMEM(ivar.shape, F32),
            pltpu.SMEM(counts.shape, jnp.int32),
            pltpu.VMEM((TILES, SLOTS, ROWS, 2 * TILE), BF16),
            pltpu.VMEM((NB, SETS, TILE), F32),
            pltpu.VMEM((TILES, TILE), jnp.int32),
            pltpu.VMEM((TILE, NB * ROWS), BF16),
            pltpu.VMEM((2 * TILE, NB * TILE), BF16),
            pltpu.VMEM((TILES, SLOTS, 24, TILE), F32),
            pltpu.VMEM((NB * ROWS, WIDE), BF16),
            pltpu.VMEM((ROWS, WIDE), BF16),
            pltpu.VMEM((ROWS, WIDE), BF16),
            pltpu.VMEM((2, WHOLE, WIDE + TILE), BF16),
            pltpu.VMEM((2, WHOLE, WIDE + TILE), BF16),
            pltpu.VMEM((2 * NEAR, WIDE), F32),
            pltpu.VMEM((2 * NEAR, WIDE), F32),
            dma((TILES,)), dma((7,)), dma((3,)), dma((3,)), dma((2,)), dma((2,)),
        ],
        compiler_params=pltpu.CompilerParams(
            collective_id=0, has_side_effects=True, vmem_limit_bytes=56 << 20),
        cost_estimate=pl.CostEstimate(flops=4_000_000_000, bytes_accessed=2_000_000, transcendentals=0),
    )(images, row_taps, col_taps, coef.transpose(2, 1, 0), blocks.T, boxes.T, ivar, counts)


def solution(mesh):
    return jax.shard_map(
        functools.partial(local_part, mesh.shape["ra"], mesh.shape["slab"]),
        mesh=mesh,
        in_specs=(P("ra", "slab", None), P(), P(), P(), P(), P(), P(), P()),
        out_specs=P("slab", "ra"),
        check_vma=False,
    )
```

profile of v0, /device:TPU:1, one launch (start us, length us, event | category | flops | bytes accessed | tf_op | source)
XLA Modules:
  0.0 22.3 jit_solution(12996587421142099232)
XLA Ops:
  0.0 21.6 %shard_map.82 = f32[64,512]{1,0:T(8,128)S(1)} custom-call(bf16[4,64,1024]{2,1,0:T(8,128)(2,1)} %images.1, bf16[20,41]{1,0:T(8,128)(2,1)} %row_taps_in.1, bf16[20,41]{1,0:T(8,128)(2,1)} %col_taps_in.1, f32[20,4,512]{2,1,0:T(4,128)} %bitcast.3, s32[8,512]{1,0:T(8,128)} %bitcast.4, s32[2,512]{1,0:T(2,128)} %bitcast.5, f32[512]{0:T(512)} %ivar_in.1, s32[128]{0:T(128)} %counts_in.1), custom_call_target="tpu_custom_call" | custom-call | flops 4000000000 | bytes 2000000 | tf_op jit(solution)/shard_map/pallas_call | solution.py:285
  21.6 0.7 %copy.10 = f32[64,512]{1,0:T(8,128)} copy(f32[64,512]{1,0:T(8,128)S(1)} %shard_map.82) | data formatting | bytes 262144
where the time goes:
time: 22.5 us; the launch traced here: 22.3 us
  Pallas kernels  21.6 us (96%)
  local copies, waits for them, and re-layouts  0.66 us (3%)
    pallas_call x1, Pallas kernels, local_part(): pl.pallas_call(functools.partial(kernel, npatch, nslab), out_shape=pltpu....  21.6 us
    unnamed x1, local copies, waits for them, and re-layouts  0.66 us

commit v1 on v0

--- a/solution.py
+++ b/solution.py
@@ -210,10 +210,10 @@
         tiles[t].wait()
     factors(0)
     spread(0)
-    filtered(0, range(0, 3), False)
+    filtered(0, range(0, 4), False)
+    send_to(3)
     send_to(2)
-    send_to(3)
-    filtered(0, range(3, 10), False)
+    filtered(0, range(4, 10), False)
     send_to(0)
     home = row_product()
     near_out[0:NEAR, :] = home[EDGE - NEAR:EDGE]

time: 22.5 us -> 22.5 us (level)
  no operation moved by 1% of the time
where the time goes in v1:
time: 22.5 us; the launch traced here: 22.3 us
  Pallas kernels  21.6 us (96%)
  local copies, waits for them, and re-layouts  0.66 us (3%)
    pallas_call x1, Pallas kernels, local_part(): pl.pallas_call(functools.partial(kernel, npatch, nslab), out_shape=pltpu....  21.6 us
    unnamed x1, local copies, waits for them, and re-layouts  0.66 us

profile of v1, /device:TPU:1, one launch (start us, length us, event | category | flops | bytes accessed | tf_op | source)
XLA Modules:
  0.0 22.3 jit_solution(14522256001350846917)
XLA Ops:
  0.0 21.6 %shard_map.82 = f32[64,512]{1,0:T(8,128)S(1)} custom-call(bf16[4,64,1024]{2,1,0:T(8,128)(2,1)} %images.1, bf16[20,41]{1,0:T(8,128)(2,1)} %row_taps_in.1, bf16[20,41]{1,0:T(8,128)(2,1)} %col_taps_in.1, f32[20,4,512]{2,1,0:T(4,128)} %bitcast.3, s32[8,512]{1,0:T(8,128)} %bitcast.4, s32[2,512]{1,0:T(2,128)} %bitcast.5, f32[512]{0:T(512)} %ivar_in.1, s32[128]{0:T(128)} %counts_in.1), custom_call_target="tpu_custom_call" | custom-call | flops 4000000000 | bytes 2000000 | tf_op jit(solution)/shard_map/pallas_call | solution.py:285
  21.7 0.7 %copy.10 = f32[64,512]{1,0:T(8,128)} copy(f32[64,512]{1,0:T(8,128)S(1)} %shard_map.82) | data formatting | bytes 262144
